TPU v7x, 32 devices: a whole 2x2x4 slice. The times are simulated.
32 devices in a mesh: img: 16 (over z, x, core), rows: 2 (over y).
Axes of the slice: x: 2, y: 2, z: 4, core: 2. Of those that a mesh axis runs over, the one named last changes fastest.
Arguments:
- inputs: float32 [16, 48, 24, 512], P('img', 'rows'), may hold values from -6 to 6
- cotangent: float32 [16, 48, 24, 512], P('img', 'rows'), may hold values from -6 to 6
- region: int32 [16, 48, 24], P('img', 'rows'), may hold values from 0 to 7, as said below
- rel_index: int32 [576, 576], replicated, may hold values from 0 to 2208, as said below
- qkv_weight: bfloat16 [2, 512, 1536], replicated, may hold values from -0.25 to 0.25
- qv_bias: float32 [2, 2, 512], replicated, may hold values from -3 to 3
- logit_scale: float32 [2, 16], replicated, may hold values from 1.8 to 2.6
- place_in: float32 [2, 2, 512], replicated, may hold values from -5 to 5
- place_bias: float32 [2, 512], replicated, may hold values from -3 to 3
- place_out: float32 [2, 512, 16], replicated, may hold values from -0.25 to 0.25
- proj_weight: bfloat16 [2, 512, 512], replicated, may hold values from -0.25 to 0.25
- up_weight: bfloat16 [2, 512, 2048], replicated, may hold values from -0.25 to 0.25
- up_bias: float32 [2, 2048], replicated, may hold values from -3 to 3
- down_weight: bfloat16 [2, 2048, 512], replicated, may hold values from -0.125 to 0.125
- out_bias: float32 [2, 2, 512], replicated, may hold values from -3 to 3
- norm_gain: float32 [2, 2, 512], replicated, may hold values from 0.5 to 1.5
- norm_shift: float32 [2, 2, 512], replicated, may hold values from -2 to 2
Outputs:
- output: float32 [16, 48, 24, 512], P('img', 'rows')
- input_grad: float32 [16, 48, 24, 512], P('img', 'rows')
- qkv_grad: float32 [2, 512, 1536], P(None, 'img', 'rows')
- qv_bias_grad: float32 [2, 2, 512], replicated
- logit_scale_grad: float32 [2, 16], replicated
- place_in_grad: float32 [2, 2, 512], replicated
- place_bias_grad: float32 [2, 512], replicated
- place_out_grad: float32 [2, 512, 16], replicated
- proj_grad: float32 [2, 512, 512], P(None, 'img', 'rows')
- up_grad: float32 [2, 512, 2048], P(None, 'img', 'rows')
- up_bias_grad: float32 [2, 2048], replicated
- down_grad: float32 [2, 2048, 512], P(None, 'img', 'rows')
- out_bias_grad: float32 [2, 2, 512], replicated
- norm_gain_grad: float32 [2, 2, 512], replicated
- norm_shift_grad: float32 [2, 2, 512], replicated
Inputs may be any that keep to these rules, and one draw needn't show every extreme that they name: `region`: in each 24-row band of an image the labels split the band at one row and one column into up to four rectangles, with labels 4 * band + 2 * (lower part) + (right part). rel_index[i, j] names the table entry of the row and column offsets between tokens i and j of a window (row-major order), the same signs or swapping for all pairs.
All inputs are finite; a program needn't handle non-finite values.
Results may differ from a plain program's by a relative error of at most 0.017.
Values may be sent and summed in bfloat16 or wider, within the bound.
A program may use at most 576 MiB of HBM per device.

v0:
```python
import jax
import jax.numpy as jnp
from jax import lax
from jax.sharding import PartitionSpec as P

HIGH = lax.Precision.HIGHEST


def passed_along(array, axis, by):
    devices = lax.axis_size(axis)
    return lax.ppermute(array, axis, [(i, (i + by) % devices) for i in range(devices)])


def table_coords(window):
    span = 2 * window - 1
    offsets = jnp.arange(span, dtype=jnp.float32) - (window - 1)
    scaled = offsets * (8.0 / (window - 1))
    logged = jnp.sign(scaled) * jnp.log2(jnp.abs(scaled) + 1.0) / 3.0
    first = jnp.repeat(logged, span)
    second = jnp.tile(logged, span)
    return jnp.stack([first, second], axis=1)


def position_bias(coords, rel_index, weight_in, bias_in, weight_out):
    hidden_net = jax.nn.gelu(
        jnp.dot(coords, weight_in, precision=HIGH) + bias_in, approximate=False
    )
    table = 16.0 * jax.nn.sigmoid(jnp.dot(hidden_net, weight_out, precision=HIGH))
    heads_first = jnp.transpose(table)
    return heads_first[:, rel_index]


def layer_norm(values, gain, shift):
    centre = values - jnp.mean(values, axis=-1, keepdims=True)
    spread = jnp.mean(centre * centre, axis=-1, keepdims=True)
    return centre * lax.rsqrt(spread + 1e-05) * gain + shift


def unit(values):
    return values * lax.rsqrt(jnp.sum(values * values, axis=-1, keepdims=True) + 1e-06)


def gelu_exact(values):
    return jax.nn.gelu(values, approximate=False)


def window_scores(queries, keys, same_mask, bias, scale_now):
    cosine = jnp.einsum("thd,shd->hts", queries, keys, preferred_element_type=jnp.float32)
    scores = cosine * scale_now[:, None, None] + bias
    if same_mask is not None:
        scores = jnp.where(same_mask[None], scores, -1000000000.0)
    return (cosine, scores)


def attend(queries, keys, values, same_mask, bias, scale_now):
    tokens = queries.shape[0]
    cosine, scores = window_scores(queries, keys, same_mask, bias, scale_now)
    top = jnp.max(scores, axis=-1, keepdims=True)
    expo = jnp.exp(scores - top)
    total = jnp.sum(expo, axis=-1, keepdims=True)
    probs = (expo / total).astype(jnp.bfloat16)
    mixed = jnp.einsum("hts,shd->thd", probs, values, preferred_element_type=jnp.float32)
    log_total = top[..., 0] + jnp.log(total[..., 0])
    return (mixed.reshape(tokens, -1).astype(jnp.bfloat16), log_total)


def attend_back(queries, keys, values, same_mask, log_total, grad_mixed, bias, scale_now):
    tokens, heads, depth = queries.shape
    cosine, scores = window_scores(queries, keys, same_mask, bias, scale_now)
    probs = jnp.exp(scores - log_total[:, :, None])
    probs_low = probs.astype(jnp.bfloat16)
    grad_heads = grad_mixed.reshape(tokens, heads, depth)
    grad_probs = jnp.einsum("thd,shd->hts", grad_heads, values, preferred_element_type=jnp.float32)
    grad_values = jnp.einsum(
        "hts,thd->shd", probs_low, grad_heads, preferred_element_type=jnp.float32
    )
    grad_scores = probs * (grad_probs - jnp.sum(grad_probs * probs, axis=-1, keepdims=True))
    grad_cos = (grad_scores * scale_now[:, None, None]).astype(jnp.bfloat16)
    grad_queries = jnp.einsum("hts,shd->thd", grad_cos, keys, preferred_element_type=jnp.float32)
    grad_keys = jnp.einsum("hts,thd->shd", grad_cos, queries, preferred_element_type=jnp.float32)
    scale_part = jnp.sum(grad_scores * cosine, axis=(1, 2)) * scale_now
    return (grad_queries, grad_keys, grad_values, grad_scores, scale_part)


def block_forward(inputs_now, layer, params, bias, same_mask, shifted):
    w_qkv, qv_bias, logit_scale, w_proj, w_up, up_bias, w_down, out_bias, norm_gain, norm_shift = (
        params
    )
    batches, height, breadth, width = inputs_now.shape
    halfway = breadth // 2
    win_tok = breadth * breadth
    heads = logit_scale.shape[1]
    low_in = inputs_now.astype(jnp.bfloat16)
    if shifted:
        incoming = passed_along(low_in[:, :halfway], "rows", -1)
        low_in = jnp.roll(
            jnp.concatenate([low_in[:, halfway:], incoming], axis=1), -halfway, axis=2
        )
    entry_flat = low_in.reshape(-1, width)
    qkv_bias = jnp.concatenate(
        [qv_bias[layer, 0], jnp.zeros_like(qv_bias[layer, 0]), qv_bias[layer, 1]]
    )
    projected = jnp.dot(entry_flat, w_qkv[layer], preferred_element_type=jnp.float32) + qkv_bias
    parts_raw = projected.reshape(-1, win_tok, 3, heads, width // heads)
    queries = unit(parts_raw[:, :, 0]).astype(jnp.bfloat16)
    keys_low = unit(parts_raw[:, :, 1]).astype(jnp.bfloat16)
    values_low = parts_raw[:, :, 2].astype(jnp.bfloat16)
    scale_now = jnp.exp(logit_scale[layer])

    def per_window(item):
        return attend(item[0], item[1], item[2], item[3], bias, scale_now)

    mixed, log_totals = lax.map(per_window, (queries, keys_low, values_low, same_mask))
    mixed = mixed.reshape(batches, height, breadth, width)
    if shifted:
        mixed = jnp.roll(mixed, halfway, axis=2)
        returned = passed_along(mixed[:, height - halfway :], "rows", 1)
        mixed = jnp.concatenate([returned, mixed[:, : height - halfway]], axis=1)
    mixed_flat = mixed.reshape(-1, width)
    attn_out = (
        jnp.dot(mixed_flat, w_proj[layer], preferred_element_type=jnp.float32) + out_bias[layer, 0]
    )
    resid = inputs_now.reshape(-1, width) + layer_norm(
        attn_out, norm_gain[layer, 0], norm_shift[layer, 0]
    )
    resid_low = resid.astype(jnp.bfloat16)
    pre_act = jnp.dot(resid_low, w_up[layer], preferred_element_type=jnp.float32) + up_bias[layer]
    act_low = gelu_exact(pre_act).astype(jnp.bfloat16)
    mlp_out = (
        jnp.dot(act_low, w_down[layer], preferred_element_type=jnp.float32) + out_bias[layer, 1]
    )
    result = resid + layer_norm(mlp_out, norm_gain[layer, 1], norm_shift[layer, 1])
    saved = (
        entry_flat,
        parts_raw,
        queries,
        keys_low,
        values_low,
        log_totals,
        mixed_flat,
        attn_out,
        resid_low,
        pre_act,
        act_low,
        mlp_out,
    )
    return (result.reshape(inputs_now.shape), saved)


def block_backward(grad_out, saved, layer, params, bias, same_mask, shifted):
    w_qkv, qv_bias, logit_scale, w_proj, w_up, up_bias, w_down, out_bias, norm_gain, norm_shift = (
        params
    )
    (
        entry_flat,
        parts_raw,
        queries,
        keys_low,
        values_low,
        log_totals,
        mixed_flat,
        attn_out,
        resid_low,
        pre_act,
        act_low,
        mlp_out,
    ) = saved
    batches, height, breadth, width = grad_out.shape
    halfway = breadth // 2
    win_tok = breadth * breadth
    heads = logit_scale.shape[1]
    grad_top = grad_out.reshape(-1, width)
    norm_pull = jax.vjp(layer_norm, mlp_out, norm_gain[layer, 1], norm_shift[layer, 1])[1]
    grad_mlp, gain_grad_two, shift_grad_two = norm_pull(grad_top)
    grad_mlp_low = grad_mlp.astype(jnp.bfloat16)
    down_grad = jnp.einsum("tf,td->fd", act_low, grad_mlp_low, preferred_element_type=jnp.float32)
    grad_act = jnp.einsum(
        "td,fd->tf", grad_mlp_low, w_down[layer], preferred_element_type=jnp.float32
    )
    grad_pre = jax.vjp(gelu_exact, pre_act)[1](grad_act)[0].astype(jnp.bfloat16)
    up_grad = jnp.einsum("td,tf->df", resid_low, grad_pre, preferred_element_type=jnp.float32)
    grad_resid = grad_top + jnp.einsum(
        "tf,df->td", grad_pre, w_up[layer], preferred_element_type=jnp.float32
    )
    attn_pull = jax.vjp(layer_norm, attn_out, norm_gain[layer, 0], norm_shift[layer, 0])[1]
    grad_attn, gain_grad_one, shift_grad_one = attn_pull(grad_resid)
    grad_attn_low = grad_attn.astype(jnp.bfloat16)
    proj_grad = jnp.einsum(
        "td,te->de", mixed_flat, grad_attn_low, preferred_element_type=jnp.float32
    )
    grad_mixed = jnp.einsum(
        "te,de->td", grad_attn_low, w_proj[layer], preferred_element_type=jnp.float32
    )
    grad_mixed = grad_mixed.astype(jnp.bfloat16).reshape(batches, height, breadth, width)
    if shifted:
        borrowed = passed_along(grad_mixed[:, :halfway], "rows", -1)
        grad_mixed = jnp.roll(
            jnp.concatenate([grad_mixed[:, halfway:], borrowed], axis=1), -halfway, axis=2
        )
    grad_mixed = grad_mixed.reshape(-1, win_tok, width)
    scale_now = jnp.exp(logit_scale[layer])

    def back_step(carry, item):
        grad_q, grad_k, grad_v, grad_s, scale_part = attend_back(
            item[0], item[1], item[2], item[3], item[4], item[5], bias, scale_now
        )
        return ((carry[0] + grad_s, carry[1] + scale_part), (grad_q, grad_k, grad_v))

    start_carry = (
        jnp.zeros((heads, win_tok, win_tok), jnp.float32),
        jnp.zeros((heads,), jnp.float32),
    )
    (bias_grad, scale_grad), (grad_q, grad_k, grad_v) = lax.scan(
        back_step, start_carry, (queries, keys_low, values_low, same_mask, log_totals, grad_mixed)
    )
    grad_q = jax.vjp(unit, parts_raw[:, :, 0])[1](grad_q)[0]
    grad_k = jax.vjp(unit, parts_raw[:, :, 1])[1](grad_k)[0]
    grad_qkv = (
        jnp.stack([grad_q, grad_k, grad_v], axis=2).reshape(-1, 3 * width).astype(jnp.bfloat16)
    )
    qkv_sums = jnp.sum(grad_qkv.astype(jnp.float32), axis=0)
    qv_grad = jnp.stack([qkv_sums[:width], qkv_sums[2 * width :]])
    qkv_grad = jnp.einsum("td,te->de", entry_flat, grad_qkv, preferred_element_type=jnp.float32)
    grad_entry = jnp.einsum("te,de->td", grad_qkv, w_qkv[layer], preferred_element_type=jnp.float32)
    if shifted:
        grad_entry = grad_entry.astype(jnp.bfloat16).reshape(batches, height, breadth, width)
        grad_entry = jnp.roll(grad_entry, halfway, axis=2)
        owned = passed_along(grad_entry[:, height - halfway :], "rows", 1)
        grad_entry = jnp.concatenate([owned, grad_entry[:, : height - halfway]], axis=1)
        grad_entry = grad_entry.astype(jnp.float32).reshape(-1, width)
    grad_in = (grad_resid + grad_entry).reshape(grad_out.shape)
    out_bias_grad = jnp.stack(
        [
            jnp.sum(grad_attn_low.astype(jnp.float32), axis=0),
            jnp.sum(grad_mlp_low.astype(jnp.float32), axis=0),
        ]
    )
    up_bias_grad = jnp.sum(grad_pre.astype(jnp.float32), axis=0)
    gain_grad = jnp.stack([gain_grad_one, gain_grad_two])
    shift_grad = jnp.stack([shift_grad_one, shift_grad_two])
    large = (qkv_grad, proj_grad, up_grad, down_grad)
    vectors = (up_bias_grad, qv_grad, out_bias_grad, gain_grad, shift_grad)
    return (grad_in, large, vectors, scale_grad, bias_grad)


def per_device(
    inputs,
    cotangent,
    region,
    rel_index,
    qkv_weight,
    qv_bias,
    logit_scale,
    place_in,
    place_bias,
    place_out,
    proj_weight,
    up_weight,
    up_bias,
    down_weight,
    out_bias,
    norm_gain,
    norm_shift,
):
    batches, height, breadth, width = inputs.shape
    params = (
        qkv_weight,
        qv_bias,
        logit_scale,
        proj_weight,
        up_weight,
        up_bias,
        down_weight,
        out_bias,
        norm_gain,
        norm_shift,
    )
    coords = table_coords(breadth)

    def bias_of(weight_in, bias_in, weight_out):
        return position_bias(coords, rel_index, weight_in, bias_in, weight_out)

    bias_zero, pull_zero = jax.vjp(bias_of, place_in[0], place_bias[0], place_out[0])
    bias_one, pull_one = jax.vjp(bias_of, place_in[1], place_bias[1], place_out[1])
    labels = region.reshape(-1, breadth * breadth)
    same_mask = labels[:, :, None] == labels[:, None, :]
    hidden, saved_zero = block_forward(inputs, 0, params, bias_zero, None, False)
    output, saved_one = block_forward(hidden, 1, params, bias_one, same_mask, True)
    grad_mid, large_one, vectors_one, scale_one, bias_grad_one = block_backward(
        cotangent, saved_one, 1, params, bias_one, same_mask, True
    )
    input_grad, large_zero, vectors_zero, scale_zero, bias_grad_zero = block_backward(
        grad_mid, saved_zero, 0, params, bias_zero, None, False
    )
    joined = tuple((jnp.stack([first, second]) for first, second in zip(large_zero, large_one)))
    partial_rows = (
        lax.psum_scatter(
            joined[0].astype(jnp.bfloat16), "rows", scatter_dimension=2, tiled=True
        ).astype(jnp.float32),
        lax.psum_scatter(
            joined[1].astype(jnp.bfloat16), "rows", scatter_dimension=2, tiled=True
        ).astype(jnp.float32),
        lax.psum_scatter(
            joined[2].astype(jnp.bfloat16), "rows", scatter_dimension=2, tiled=True
        ).astype(jnp.float32),
        lax.psum_scatter(
            joined[3].astype(jnp.bfloat16), "rows", scatter_dimension=2, tiled=True
        ).astype(jnp.float32),
    )
    stacked = (
        lax.psum_scatter(partial_rows[0], "img", scatter_dimension=1, tiled=True),
        lax.psum_scatter(partial_rows[1], "img", scatter_dimension=1, tiled=True),
        lax.psum_scatter(partial_rows[2], "img", scatter_dimension=1, tiled=True),
        lax.psum_scatter(partial_rows[3], "img", scatter_dimension=1, tiled=True),
    )
    net_zero = pull_zero(bias_grad_zero)
    net_one = pull_one(bias_grad_one)
    vector_pairs = tuple(
        (jnp.stack([first, second]) for first, second in zip(vectors_zero, vectors_one))
    )
    small = (
        jnp.stack([scale_zero, scale_one]),
        jnp.stack([net_zero[0], net_one[0]]),
        jnp.stack([net_zero[1], net_one[1]]),
        jnp.stack([net_zero[2], net_one[2]]),
    ) + vector_pairs
    summed_small = lax.psum(small, ("img", "rows"))
    (
        scale_grad,
        place_in_grad,
        place_bias_grad,
        place_out_grad,
        up_bias_grad,
        qv_grad,
        out_bias_grad,
        gain_grad,
        shift_grad,
    ) = summed_small
    qkv_grad, proj_grad, up_grad, down_grad = stacked
    return (
        output,
        input_grad,
        qkv_grad,
        qv_grad,
        scale_grad,
        place_in_grad,
        place_bias_grad,
        place_out_grad,
        proj_grad,
        up_grad,
        up_bias_grad,
        down_grad,
        out_bias_grad,
        gain_grad,
        shift_grad,
    )


def solution(mesh):
    placed = (
        P("img", "rows", None, None),
        P("img", "rows", None, None),
        P("img", "rows", None),
        P(),
        P(),
        P(),
        P(),
        P(),
        P(),
        P(),
        P(),
        P(),
        P(),
        P(),
        P(),
        P(),
        P(),
    )
    return jax.shard_map(
        per_device,
        mesh=mesh,
        in_specs=placed,
        out_specs=(
            P("img", "rows", None, None),
            P("img", "rows", None, None),
            P(None, "img", "rows"),
            P(),
            P(),
            P(),
            P(),
            P(),
            P(None, "img", "rows"),
            P(None, "img", "rows"),
            P(),
            P(None, "img", "rows"),
            P(),
            P(),
            P(),
        ),
        check_vma=False,
    )
```

profile of v0, /device:TPU:0, one launch (start us, length us, event | category | flops | bytes accessed | tf_op | source)
XLA Modules:
  0.0 6860.5 jit_solution(4049231096486675666)
XLA Ops:
  17.0 13.3 fusion.35
  30.4 4.2 fusion.52
  35.7 1088.4 %gather_fusion = f32[331776,16]{1,0:T(8,128)} fusion(f32[16,2209]{0,1:T(8,128)S(1)} %copy.84, s32[331776]{0:T(1024)S(1)} %broadcast_clamp_fusion), kind=kCustom, calls=%fused_computation | custom fusion | bytes 43794432 | tf_op jit(solution)/shard_map/jvp()/gather | solution.py:30
  1124.0 97.0 %copy.86 = f32[576,576,16]{0,1,2:T(8,128)} copy(f32[576,576,16]{2,1,0:T(8,128)} %bitcast.14) | data formatting | bytes 42467328 | tf_op jit(solution)/shard_map/jvp()/gather | solution.py:30
  1222.0 2.5 convolution_add_fusion.3
  1224.5 3.2 copy.83
  1230.4 20.8 fusion.250
  1251.3 7.8 copy-done
  1259.1 3.5 fusion.5
  1262.7 11.9 fusion.106
  1277.9 13.1 multiply_convert_fusion.3
  1293.3 3.0 collective-permute-start
  1296.3 13.4 fusion.36
  1309.8 4.2 fusion.49
  1315.1 1088.4 %gather_fusion.1 = f32[331776,16]{1,0:T(8,128)} fusion(f32[16,2209]{0,1:T(8,128)S(1)} %copy.89, s32[331776]{0:T(1024)S(1)} %copy-done.13), kind=kCustom, calls=%fused_computation.1 | custom fusion | bytes 43794432 | tf_op jit(solution)/shard_map/jvp()/gather | solution.py:30
  2403.4 97.0 %copy.91 = f32[576,576,16]{0,1,2:T(8,128)} copy(f32[576,576,16]{2,1,0:T(8,128)} %bitcast.42) | data formatting | bytes 42467328 | tf_op jit(solution)/shard_map/jvp()/gather | solution.py:30
  2502.6 2.5 convolution_add_fusion.2
  2505.1 3.1 copy.88
  2511.0 22.9 fusion.247
  2533.9 7.8 copy-done.1
  2541.6 3.5 fusion.6
  2545.2 11.9 fusion.143
  2557.1 2.6 copy.93
  2559.7 3.9 convert_element_type.276
  2564.2 8.3 collective-permute-done.1
  2575.0 11.5 multiply_convert_fusion.2
  2591.7 3.7 convert_reduce_fusion
  2600.9 6.6 collective-permute-done.2
  2607.7 2.4 reshape.749
  2610.1 2.6 copy.94
  2612.8 11.1 fusion.140
  2623.9 42.0 multiply_reduce_fusion
  2665.9 8.3 convolution_bitcast_fusion.2
  2674.3 4.5 fusion.132
  2683.1 2.6 fusion.58
  2685.7 3.5 collective-permute-done.3
  2691.9 7.1 convert_reduce_fusion.1
  2699.1 2.4 multiply_reduce_fusion.10
  2704.0 11.1 fusion.137
  2715.1 42.2 multiply_reduce_fusion.1
  2757.3 8.3 convolution_bitcast_fusion
  2765.7 4.6 fusion.136
  2780.5 3.6 fusion.54
  2786.0 2.3 pad_maximum_fusion
  2788.7 3.6 fusion.56
  2794.2 2.4 pad_maximum_fusion.1
  2796.6 24.2 reduce-scatter.8.cloned.1.call-done
  2820.8 5.2 copy.104
  2826.1 84.1 %copy.126 = f32[576,576,16]{2,1,0:T(8,128)} copy(f32[576,576,16]{0,1,2:T(8,128)} %bitcast.403) | data formatting | bytes 42467328 | tf_op jit(solution)/shard_map/while/body/eval_jaxpr/mul | solution.py:77
  2910.3 1755.2 %scatter_custom_fusion.1 = f32[16,2209]{0,1:T(8,128)S(1)} fusion(s32[331776]{0:T(1024)} %reshape.766, f32[331776,16]{1,0:T(8,128)} %bitcast.89, f32[]{:T(128)} %constant.62.clone.1), kind=kCustom, calls=%fused_computation.296 | custom fusion | flops 5308416 | bytes 141888 | tf_op jit(solution)/shard_map/transpose(jvp())/scatter-add | solution.py:30
  4665.8 6.8 fusion.151
  4672.5 84.0 %copy.125 = f32[576,576,16]{2,1,0:T(8,128)} copy(f32[576,576,16]{0,1,2:T(8,128)} %bitcast.404) | data formatting | bytes 42467328 | tf_op jit(solution)/shard_map/while/body/eval_jaxpr/mul | solution.py:77
  4756.6 1755.0 %scatter_custom_fusion = f32[16,2209]{0,1:T(8,128)S(1)} fusion(s32[331776]{0:T(1024)} %reshape.766, f32[331776,16]{1,0:T(8,128)} %bitcast.85, f32[]{:T(128)} %constant.62.clone.1), kind=kCustom, calls=%fused_computation.298 | custom fusion | flops 5308416 | bytes 141888 | tf_op jit(solution)/shard_map/transpose(jvp())/scatter-add | solution.py:30
  6511.9 6.8 fusion.152
  6521.6 4.0 convert_element_type.300
  6526.0 4.0 convert_element_type.303
  6531.6 13.8 fusion.275
  6547.9 14.1 fusion.276
  6564.7 40.9 all-reduce.1
  6605.7 3.8 fusion.107
  6611.1 25.9 all-reduce.5.cloned.1.call-done
  6637.0 62.4 reduce-scatter.12.cloned.1.call-done
  6699.4 76.3 %reduce-scatter.16.cloned.1.call-done = f32[2,32,1024]{2,1,0:T(8,128)} async-done(((f32[2,512,1024]{2,1,0:T(8,128)}), f32[2,32,1024]{2,1,0:T(8,128)}) %reduce-scatter.16.cloned.1.call-update) | async-done | bytes 262160 | tf_op jit(solution)/shard_map/reduce_scatter | solution.py:313
  6775.7 76.2 %reduce-scatter.20.cloned.1.call-done = f32[2,128,256]{2,1,0:T(8,128)} async-done(((f32[2,2048,256]{2,1,0:T(8,128)}), f32[2,128,256]{2,1,0:T(8,128)}) %reduce-scatter.20.cloned.1.call-update) | async-done | bytes 262160 | tf_op jit(solution)/shard_map/reduce_scatter | solution.py:314
  (467 shorter events, 75.7 us)
Async XLA Ops:
  7.2 9.8 copy-start.145
  7.2 2813.6 %reduce-scatter.8.cloned.1.call-start = ((), (), s32[]{:S(2)}) async-start(), calls=%async_computation.7 | async-start | bytes 4718592 | tf_op jit(solution)/shard_map/reduce_scatter | solution.py:297
  11.5 18.9 copy-start.75
  11.7 18.7 copy-start.78
  16.4 19.2 copy-start.12
  17.0 13.4 copy-start.83
  1124.0 97.0 %copy-start.27 = (f32[1,24,24,512]{3,2,1,0:T(8,128)S(1)}, f32[1,24,24,512]{3,2,1,0:T(8,128)}, u32[]{:S(2)}) copy-start(f32[1,24,24,512]{3,2,1,0:T(8,128)} %param.17) | copy-start | bytes 3538948
  1124.0 97.1 %copy-start.112 = (f32[2,2,512]{2,1,0:T(2,128)S(1)}, f32[2,2,512]{2,1,0:T(2,128)}, u32[]{:S(2)}) copy-start(f32[2,2,512]{2,1,0:T(2,128)} %param.22) | copy-start | bytes 24580
  1229.8 21.4 copy-start.32
  1230.4 20.8 copy-start.43
  1251.2 11.4 copy-start.59
  1262.6 12.0 copy-start.69
  1262.6 12.0 copy-start.113
  1262.6 12.6 copy-start.114
  1262.6 13.2 copy-start.133
  1262.6 13.2 copy-start.142
  1274.6 16.3 copy-start.147
  1275.2 17.6 copy-start.102
  1275.8 17.1 copy-start.88
  1277.8 15.1 copy-start.20
  1277.8 13.1 copy-start.132
  1277.8 13.1 copy-start.136
  1292.5 17.3 copy-start.6
  1292.5 17.2 copy-start.71
  1292.8 16.9 copy-start.92
  1292.9 16.9 copy-start.73
  1293.3 1208.3 %collective-permute-start = (bf16[1,12,24,512]{3,2,1,0:T(8,128)(2,1)S(1)}, bf16[1,12,24,512]{3,2,1,0:T(8,128)(2,1)S(1)}, u32[]{:S(2)}, u32[]{:S(2)}) collective-permute-start(bf16[1,12,24,512]{3,2,1,0:T(8,128)(2,1)S(1)} %get-tuple-element.261), channel_id=1, source_target_pairs={{0,1},{1,0},{2,3},{3,2},{4,5},{5,4},{6,7},{7,6},{8,9},{9,8},{10,11... | collective-permute-start | bytes 884744 | tf_op jit(solution)/shard_map/ppermute | solution.py:11
  1296.3 13.5 copy-start.84
  2403.4 97.0 %copy-start.105 = (s32[1,24,24]{2,1,0:T(8,128)S(1)}, s32[1,24,24]{2,1,0:T(8,128)}, u32[]{:S(2)}) copy-start(s32[1,24,24]{2,1,0:T(8,128)} %param.19) | copy-start | bytes 6916
  2403.4 99.2 %copy-start.115 = (f32[1536]{0:T(1024)S(1)}, f32[1536]{0:T(1024)}, u32[]{:S(2)}) copy-start(f32[1536]{0:T(1024)} %get-tuple-element.286) | copy-start | bytes 18436
  2510.4 23.5 copy-start.34
  2511.0 22.9 copy-start.45
  2559.7 12.9 copy-start.131
  2563.8 9.7 copy-start.7
  2563.8 9.7 copy-start.21
  2563.8 9.7 copy-start.72
  2563.8 9.7 copy-start.74
  2563.8 9.7 copy-start.89
  2563.8 9.7 copy-start.101
  2563.8 9.7 copy-start.103
  2564.0 8.5 collective-permute-start.1
  2574.1 15.3 copy-start.25
  2575.0 11.5 copy-start.130
  2575.0 11.5 copy-start.137
  2597.7 9.9 copy-start.18
  2599.8 7.6 collective-permute-start.2
  2623.9 42.0 copy-start.46
  2682.4 6.8 collective-permute-start.3
  2704.0 11.2 copy-start.97
  2715.1 42.2 copy-start.44
  2777.0 3742.4 %reduce-scatter.10.cloned.1.call-start = ((), (), s32[]{:S(2)}) async-start(), calls=%async_computation.9 | async-start | bytes 1572864 | tf_op jit(solution)/shard_map/reduce_scatter | solution.py:300
  2780.4 3741.1 %reduce-scatter.14.cloned.1.call-start = ((), (), s32[]{:S(2)}) async-start(), calls=%async_computation.11 | async-start | bytes 6291456 | tf_op jit(solution)/shard_map/reduce_scatter | solution.py:303
  2788.4 3737.6 %reduce-scatter.18.cloned.1.call-start = ((), (), s32[]{:S(2)}) async-start(), calls=%async_computation.13 | async-start | bytes 6291456 | tf_op jit(solution)/shard_map/reduce_scatter | solution.py:306
  2796.6 3812.9 %all-reduce.7.cloned.1.call-start = ((), (), s32[]{:S(2)}) async-start(), calls=%async_computation.15 | async-start | bytes 6291456
  2826.1 3810.9 %all-reduce.5.cloned.1.call-start = ((), (), s32[]{:S(2)}) async-start(), calls=%async_computation.8 | async-start | bytes 131072 | tf_op jit(solution)/shard_map/psum | solution.py:327
  2826.1 1839.6 %copy-start.39 = (f32[2209,16]{0,1:T(8,128)S(1)}, f32[2209,16]{0,1:T(8,128)}, u32[]{:S(2)}) copy-start(f32[2209,16]{0,1:T(8,128)} %copy-done.38) | copy-start | bytes 424132
  4672.5 1839.3 %copy-start.37 = (f32[2209,16]{0,1:T(8,128)S(1)}, f32[2209,16]{0,1:T(8,128)}, u32[]{:S(2)}) copy-start(f32[2209,16]{0,1:T(8,128)} %copy-done.36) | copy-start | bytes 424132
  6519.3 180.1 %reduce-scatter.12.cloned.1.call-start = ((), (), s32[]{:S(2)}) async-start(), calls=%async_computation.10 | async-start | bytes 1114112 | tf_op jit(solution)/shard_map/reduce_scatter | solution.py:312
  6521.5 254.2 %reduce-scatter.16.cloned.1.call-start = ((), (), s32[]{:S(2)}) async-start(), calls=%async_computation.12 | async-start | bytes 4456448 | tf_op jit(solution)/shard_map/reduce_scatter | solution.py:313
  6525.7 326.3 %reduce-scatter.20.cloned.1.call-start = ((), (), s32[]{:S(2)}) async-start(), calls=%async_computation.14 | async-start | bytes 4456448 | tf_op jit(solution)/shard_map/reduce_scatter | solution.py:314
  6531.6 13.9 copy-start.77
  6531.6 13.9 copy-start.80
  6562.2 43.5 copy-start.30
  6562.2 43.5 copy-start.41
  (104 other events, 382.6 us)
Sparse Core Ops, SparseCore 0:
  2777.1 43.6 reduce-scatter.7
  2823.1 20.3 reduce-scatter.9
  2845.8 54.2 reduce-scatter.13
  2902.4 54.3 reduce-scatter.17
  2960.1 103.5 all-reduce.6
  6519.4 117.5 all-reduce.4
  6641.2 58.1 reduce-scatter.11
  6704.4 71.3 reduce-scatter.15
  6780.2 71.7 reduce-scatter.19
where the time goes:
time: 6880 us; the launch traced here: 6860 us
  other arithmetic  3560 us (52%)
  local copies, waits for them, and re-layouts  2600 us (38%)
  matrix products  353 us (5%)
  waiting for transfers between devices  284 us (4%)
    scatter-add x2, other arithmetic, position_bias(): return heads_first[:, rel_index]  3510 us
    gather x4, local copies, waits for them, and re-layouts, position_bias(): return heads_first[:, rel_index]  2370 us
    mul x2, local copies, waits for them, and re-layouts, attend_back(): probs * (grad_probs - jnp.sum(grad_probs * probs, axis=-1, keepdims=True))  168 us
  transfers between devices with their start and end apart: 13, of which 8 were waited for; matrix products, arithmetic and copies ran while one was open for 73% of the time, Pallas kernels for 0%

commit v1 on v0

v1 whole, which is shorter than its diff:
```python
import functools

import jax
import jax.numpy as jnp
from jax import lax
from jax.experimental import pallas as pl
from jax.experimental.pallas import tpu as pltpu
from jax.sharding import PartitionSpec as P

BF = jnp.bfloat16
F32 = jnp.float32
LOG2E = 1.4426950408889634
MASKED = 1.0e9
LANES = 128


def passed_along(array, axis, by):
    devices = lax.axis_size(axis)
    return lax.ppermute(array, axis, [(i, (i + by) % devices) for i in range(devices)])


def mm(a, b):
    return lax.dot_general(a, b, (((1,), (0,)), ((), ())), preferred_element_type=F32)


def mm_nt(a, b):
    return lax.dot_general(a, b, (((1,), (1,)), ((), ())), preferred_element_type=F32)


def mm_tn(a, b):
    return lax.dot_general(a, b, (((0,), (0,)), ((), ())), preferred_element_type=F32)


def group_sum(values, depth):
    rows = lax.broadcasted_iota(jnp.int32, (LANES, LANES), 0) // depth
    cols = lax.broadcasted_iota(jnp.int32, (LANES, LANES), 1) // depth
    ones = jnp.where(rows == cols, 1.0, 0.0).astype(BF)
    high = values.astype(BF)
    low = (values - high.astype(F32)).astype(BF)
    return mm(high, ones) + mm(low, ones)


def normal_parts(values):
    gauss = jnp.exp2(values * values * (-0.5 * LOG2E))
    size = jnp.abs(values)
    t = 1.0 / (1.0 + size * (0.3275911 * 0.7071067811865476))
    poly = t * (
        0.127414796
        + t * (-0.142248368 + t * (0.7107068705 + t * (-0.7265760135 + t * 0.5307027145)))
    )
    tail = poly * gauss
    cdf = jnp.where(values >= 0.0, 1.0 - tail, tail)
    return cdf, gauss * 0.3989422804014327


def norm_stats(values):
    centre = values - jnp.mean(values, axis=-1, keepdims=True)
    spread = jnp.mean(centre * centre, axis=-1, keepdims=True)
    rstd = lax.rsqrt(spread + 1e-05)
    return centre * rstd, rstd


def norm_pull(values, gain, grad):
    hat, rstd = norm_stats(values)
    scaled = grad * gain
    first = jnp.mean(scaled, axis=-1, keepdims=True)
    second = jnp.mean(scaled * hat, axis=-1, keepdims=True)
    pulled = rstd * (scaled - first - hat * second)
    gain_grad = jnp.sum(grad * hat, axis=0, keepdims=True)
    shift_grad = jnp.sum(grad, axis=0, keepdims=True)
    return pulled, gain_grad, shift_grad


Q_BIAS, K_BIAS, V_BIAS, OUT0, GAIN0, SHIFT0, OUT1, GAIN1, SHIFT1, SCALE = range(10)


def forward_kernel(
    masked, window, depth, groups, chunks,
    x_ref, qm_ref, km_ref, wq_ref, wk_ref, wv_ref, vec_ref, gvec_ref, bias_ref,
    wp_ref, wu_ref, wd_ref, ub_ref,
    out_ref, e_ref, qn_ref, kn_ref, v_ref, o_ref, iq_ref, ik_ref, rinv_ref, p_ref,
    a_ref, zr_ref, g_ref, gd_ref, m_ref,
    o_s, z_s, m_s,
):
    step = pl.program_id(0)
    tokens = window * window
    per = LANES // depth
    lane = lax.broadcasted_iota(jnp.int32, (1, LANES), 1) // depth

    @pl.when(step == 0)
    def _():
        e_ref[...] = x_ref[...].astype(BF)

    @pl.when(step < groups)
    def _():
        entry = e_ref[...]
        q = mm(entry, wq_ref[0]) + gvec_ref[Q_BIAS : Q_BIAS + 1]
        k = mm(entry, wk_ref[0])
        v = mm(entry, wv_ref[0]) + gvec_ref[V_BIAS : V_BIAS + 1]
        iq = lax.rsqrt(group_sum(q * q, depth) + 1e-06)
        ik = lax.rsqrt(group_sum(k * k, depth) + 1e-06)
        qn = q * iq
        kn = (k * ik).astype(BF)
        iq_ref[...] = iq
        ik_ref[...] = ik
        qn_ref[...] = qn.astype(BF)
        kn_ref[...] = kn
        v_ref[...] = v.astype(BF)
        rhs = jnp.concatenate([kn, km_ref[...]], axis=1) if masked else kn
        total = jnp.zeros((tokens, 2 * LANES), F32)
        for h in range(per):
            mine = lane == h
            lhs = jnp.where(mine, qn, 0.0).astype(BF)
            if masked:
                lhs = jnp.concatenate([lhs, qm_ref[...]], axis=1)
            cosine = mm_nt(lhs, rhs)
            scale = gvec_ref[SCALE : SCALE + 1, h * depth : h * depth + 1] * LOG2E
            table = bias_ref[h]
            for pair in range(window // 2):
                parts = []
                for r in (2 * pair, 2 * pair + 1):
                    at = window * (window - 1 - r)
                    parts.append(
                        cosine[r * window : (r + 1) * window] * scale + table[:, at : at + tokens]
                    )
                both = jnp.concatenate(parts, axis=0)
                p_ref[h, 2 * pair * window : (2 * pair + 2) * window, :] = jnp.exp2(both).astype(BF)
            weights = jnp.concatenate(
                [jnp.where(mine, v, 0.0), jnp.where(mine, jnp.ones_like(v), 0.0)], axis=1
            ).astype(BF)
            total = total + mm(p_ref[h], weights)
        rinv = 1.0 / total[:, LANES:]
        rinv_ref[...] = rinv
        o32 = total[:, :LANES] * rinv
        o_ref[...] = o32
        o = o32.astype(BF)
        o_s[:, pl.ds(pl.multiple_of(step * LANES, LANES), LANES)] = o

    @pl.when(step == groups)
    def _():
        a = mm(o_s[...], wp_ref[0]) + vec_ref[OUT0 : OUT0 + 1]
        a_ref[...] = a
        hat, _ = norm_stats(a)
        z = x_ref[...] + (hat * vec_ref[GAIN0 : GAIN0 + 1] + vec_ref[SHIFT0 : SHIFT0 + 1])
        z_s[...] = z
        zr_ref[...] = z.astype(BF)
        m_s[...] = jnp.zeros_like(m_s)

    @pl.when(step >= groups)
    def _():
        pre = mm(zr_ref[...], wu_ref[0]) + ub_ref[0]
        cdf, density = normal_parts(pre)
        act = (pre * cdf).astype(BF)
        g_ref[...] = act
        gd_ref[...] = (cdf + pre * density).astype(BF)
        m_s[...] += mm(act, wd_ref[0])

    @pl.when(step == groups + chunks - 1)
    def _():
        m = m_s[...] + vec_ref[OUT1 : OUT1 + 1]
        m_ref[...] = m
        hat, _ = norm_stats(m)
        out_ref[...] = z_s[...] + (hat * vec_ref[GAIN1 : GAIN1 + 1] + vec_ref[SHIFT1 : SHIFT1 + 1])


def block_forward(layer, x, vec, tables, labels_low, w_qkv, w_proj, w_up, up_bias, w_down, window, heads):
    tokens, width = x.shape
    depth = width // heads
    ff = w_up.shape[2]
    groups = width // LANES
    per = LANES // depth
    chunk = 512
    chunks = ff // chunk
    masked = labels_low is not None
    if masked:
        queries_mask, keys_mask = labels_low
    else:
        queries_mask = jnp.zeros((16, LANES), BF)
        keys_mask = queries_mask
    at_group = lambda s: jnp.minimum(s, groups - 1)
    at_chunk = lambda s: jnp.maximum(s - groups, 0)
    whole = lambda shape: pl.BlockSpec(shape, lambda s: (0,) * len(shape))
    by_group = pl.BlockSpec((tokens, LANES), lambda s: (0, at_group(s)))
    by_chunk = pl.BlockSpec((tokens, chunk), lambda s: (0, at_chunk(s)))
    kernel = functools.partial(forward_kernel, masked, window, depth, groups, chunks)
    tok = lambda dt, cols=width: jax.ShapeDtypeStruct((tokens, cols), dt)
    return pl.pallas_call(
        kernel,
        grid=(groups + chunks,),
        in_specs=[
            whole((tokens, width)),
            whole(queries_mask.shape),
            whole(keys_mask.shape),
            pl.BlockSpec((1, width, LANES), lambda s: (layer, 0, at_group(s))),
            pl.BlockSpec((1, width, LANES), lambda s: (layer, 0, groups + at_group(s))),
            pl.BlockSpec((1, width, LANES), lambda s: (layer, 0, 2 * groups + at_group(s))),
            whole(vec.shape),
            pl.BlockSpec((vec.shape[0], LANES), lambda s: (0, at_group(s))),
            pl.BlockSpec((per,) + tables.shape[1:], lambda s: (at_group(s), 0, 0)),
            pl.BlockSpec((1, width, width), lambda s: (layer, 0, 0)),
            pl.BlockSpec((1, width, chunk), lambda s: (layer, 0, at_chunk(s))),
            pl.BlockSpec((1, chunk, width), lambda s: (layer, at_chunk(s), 0)),
            pl.BlockSpec((1, 1, chunk), lambda s: (layer, 0, at_chunk(s))),
        ],
        out_specs=[
            whole((tokens, width)),
            whole((tokens, width)),
            by_group, by_group, by_group, by_group, by_group, by_group, by_group,
            pl.BlockSpec((per, tokens, tokens), lambda s: (at_group(s), 0, 0)),
            whole((tokens, width)),
            whole((tokens, width)),
            by_chunk, by_chunk,
            whole((tokens, width)),
        ],
        out_shape=[
            tok(F32), tok(BF),
            tok(BF), tok(BF), tok(BF), tok(F32), tok(F32), tok(F32), tok(F32),
            jax.ShapeDtypeStruct((heads, tokens, tokens), BF),
            tok(F32), tok(BF), tok(BF, ff), tok(BF, ff), tok(F32),
        ],
        scratch_shapes=[
            pltpu.VMEM((tokens, width), BF),
            pltpu.VMEM((tokens, width), F32),
            pltpu.VMEM((tokens, width), F32),
        ],
        compiler_params=pltpu.CompilerParams(vmem_limit_bytes=56 * 2**20),
        name="block_forward_%d" % layer,
    )(x, queries_mask, keys_mask, w_qkv, w_qkv, w_qkv, vec, vec, tables, w_proj, w_up, w_down, up_bias)


def feed_back_kernel(
    chunks,
    dy_ref, m_ref, a_ref, zr_ref, o_ref, g_ref, gd_ref, vec_ref, wd_ref, wu_ref, wp_ref,
    down_ref, up_ref, ub_ref, proj_ref, do_ref, dz_ref, sums_ref,
    dm_s, acc_s,
):
    step = pl.program_id(0)

    @pl.when(step == 0)
    def _():
        dm, gain_grad, shift_grad = norm_pull(m_ref[...], vec_ref[GAIN1 : GAIN1 + 1], dy_ref[...])
        low = dm.astype(BF)
        dm_s[...] = low
        sums_ref[...] = jnp.zeros_like(sums_ref)
        sums_ref[0:1] = jnp.sum(low.astype(F32), axis=0, keepdims=True)
        sums_ref[1:2] = gain_grad
        sums_ref[2:3] = shift_grad
        acc_s[...] = dy_ref[...]

    dm = dm_s[...]
    down_ref[...] = mm_tn(g_ref[...], dm).astype(BF)
    dh = (mm_nt(dm, wd_ref[0]) * gd_ref[...].astype(F32)).astype(BF)
    ub_ref[0] = jnp.sum(dh.astype(F32), axis=0, keepdims=True)
    up_ref[...] = mm_tn(zr_ref[...], dh).astype(BF)
    acc_s[...] += mm_nt(dh, wu_ref[0])

    @pl.when(step == chunks - 1)
    def _():
        dz = acc_s[...]
        dz_ref[...] = dz
        da, gain_grad, shift_grad = norm_pull(a_ref[...], vec_ref[GAIN0 : GAIN0 + 1], dz)
        low = da.astype(BF)
        sums_ref[3:4] = jnp.sum(low.astype(F32), axis=0, keepdims=True)
        sums_ref[4:5] = gain_grad
        sums_ref[5:6] = shift_grad
        proj_ref[...] = mm_tn(o_ref[...].astype(BF), low).astype(BF)
        do_ref[...] = mm_nt(low, wp_ref[0]).astype(BF)


def feed_backward(layer, dy, m, a, zr, o, g, gd, vec, w_down, w_up, w_proj):
    tokens, width = dy.shape
    ff = g.shape[1]
    chunk = 512
    chunks = ff // chunk
    whole = lambda shape: pl.BlockSpec(shape, lambda s: (0,) * len(shape))
    full = whole((tokens, width))
    by_chunk = pl.BlockSpec((tokens, chunk), lambda s: (0, s))
    sds = jax.ShapeDtypeStruct
    return pl.pallas_call(
        functools.partial(feed_back_kernel, chunks),
        grid=(chunks,),
        in_specs=[
            full, full, full, full, full, by_chunk, by_chunk, whole(vec.shape),
            pl.BlockSpec((1, chunk, width), lambda s: (layer, s, 0)),
            pl.BlockSpec((1, width, chunk), lambda s: (layer, 0, s)),
            pl.BlockSpec((1, width, width), lambda s: (layer, 0, 0)),
        ],
        out_specs=[
            pl.BlockSpec((chunk, width), lambda s: (s, 0)),
            pl.BlockSpec((width, chunk), lambda s: (0, s)),
            pl.BlockSpec((1, 1, chunk), lambda s: (0, 0, s)),
            whole((width, width)),
            full, full, whole((8, width)),
        ],
        out_shape=[
            sds((ff, width), BF), sds((width, ff), BF), sds((1, 1, ff), F32), sds((width, width), BF),
            sds((tokens, width), BF), sds((tokens, width), F32), sds((8, width), F32),
        ],
        scratch_shapes=[pltpu.VMEM((tokens, width), BF), pltpu.VMEM((tokens, width), F32)],
        compiler_params=pltpu.CompilerParams(vmem_limit_bytes=56 * 2**20),
        name="feed_backward_%d" % layer,
    )(dy, m, a, zr, o, g, gd, vec, w_down, w_up, w_proj)


def attend_back_kernel(
    window, depth, groups,
    e_ref, do_ref, o_ref, qn_ref, kn_ref, v_ref, iq_ref, ik_ref, rinv_ref, p_ref, gvec_ref,
    wq_ref, wk_ref, wv_ref, dz_ref,
    dx_ref, grads_ref, sums_ref, table_ref,
    et_s, ds_s,
):
    step = pl.program_id(0)
    tokens = window * window
    per = LANES // depth
    lane = lax.broadcasted_iota(jnp.int32, (1, LANES), 1)

    @pl.when(step == 0)
    def _():
        et_s[...] = e_ref[...].T
        dx_ref[...] = dz_ref[...]

    scale = gvec_ref[SCALE : SCALE + 1]
    v = v_ref[...]
    kn = kn_ref[...]
    qn = qn_ref[...]
    dor = (do_ref[...].astype(F32) * rinv_ref[...]).astype(BF)
    dor32 = dor.astype(F32)
    less = -group_sum(dor32 * o_ref[...], depth)
    high = less.astype(BF).astype(F32)
    extra = jnp.where(lane % depth == 0, high, jnp.where(lane % depth == 1, less - high, 0.0))
    dor_t = dor.T
    qn_t = qn.T
    rhs = jnp.concatenate([v, jnp.ones_like(v)], axis=1)
    wide = table_ref.shape[2]
    shifted = (tokens + LANES - 1) // LANES * LANES + LANES
    dq = jnp.zeros((tokens, LANES), F32)
    dk_t = []
    dv_t = []
    for h in range(per):
        mine = lane // depth == h
        lhs = jnp.concatenate(
            [jnp.where(mine, dor32, 0.0), jnp.where(mine, extra, 0.0)], axis=1
        ).astype(BF)
        t = mm_nt(lhs, rhs)
        table_ref[h] = jnp.zeros(table_ref.shape[1:], F32)
        for pair in range(window // 2):
            rows = slice(2 * pair * window, (2 * pair + 2) * window)
            ds = p_ref[h, rows, :].astype(F32) * t[rows]
            ds_s[h, rows, :] = ds.astype(BF)
            for i in range(2):
                at = window * (window - 1 - (2 * pair + i))
                block = ds[i * window : (i + 1) * window]
                table_ref[h, :, at : at + tokens] += block
        low = ds_s[h]
        keys = jnp.where(mine, kn.astype(F32), 0.0).astype(BF)
        dq = dq + mm(low, keys)
        dk_t.append(mm(qn_t[h * depth : (h + 1) * depth], low))
        dv_t.append(mm(dor_t[h * depth : (h + 1) * depth], p_ref[h]))
    dqn = dq * scale
    dkn = jnp.concatenate(dk_t, axis=0).T * scale
    dv = jnp.concatenate(dv_t, axis=0).T
    qn32 = qn.astype(F32)
    kn32 = kn.astype(F32)
    along_q = qn32 * dqn
    dq = iq_ref[...] * (dqn - qn32 * group_sum(along_q, depth))
    dk = ik_ref[...] * (dkn - kn32 * group_sum(kn32 * dkn, depth))
    sums_ref[...] = jnp.zeros_like(sums_ref)
    sums_ref[0:1] = jnp.sum(along_q, axis=0, keepdims=True)
    parts = []
    for i, part in enumerate((dq, dk, dv)):
        low = part.astype(BF)
        parts.append(low)
        sums_ref[i + 1 : i + 2] = jnp.sum(low.astype(F32), axis=0, keepdims=True)
    low = jnp.concatenate(parts, axis=1)
    grads = mm(et_s[...], low)
    for i in range(3):
        grads_ref[i] = grads[:, i * LANES : (i + 1) * LANES].astype(BF)
    weights = jnp.concatenate([wq_ref[0], wk_ref[0], wv_ref[0]], axis=1)
    dx_ref[...] += mm_nt(low, weights)


def attend_backward(layer, entry, do, saved, vec, w_qkv, dz, table_shape, window, heads):
    qn, kn, v, o, iq, ik, rinv, p = saved
    tokens, width = entry.shape
    depth = width // heads
    groups = width // LANES
    per = LANES // depth
    whole = lambda shape: pl.BlockSpec(shape, lambda s: (0,) * len(shape))
    by_group = pl.BlockSpec((tokens, LANES), lambda s: (0, s))
    full = whole((tokens, width))
    sds = jax.ShapeDtypeStruct
    return pl.pallas_call(
        functools.partial(attend_back_kernel, window, depth, groups),
        grid=(groups,),
        in_specs=[full] + [by_group] * 8 + [
            pl.BlockSpec((per, tokens, tokens), lambda s: (s, 0, 0)),
            pl.BlockSpec((vec.shape[0], LANES), lambda s: (0, s)),
            pl.BlockSpec((1, width, LANES), lambda s: (layer, 0, s)),
            pl.BlockSpec((1, width, LANES), lambda s: (layer, 0, groups + s)),
            pl.BlockSpec((1, width, LANES), lambda s: (layer, 0, 2 * groups + s)),
            full,
        ],
        out_specs=[
            full,
            pl.BlockSpec((3, width, LANES), lambda s: (0, 0, s)),
            pl.BlockSpec((8, LANES), lambda s: (0, s)),
            pl.BlockSpec((per,) + table_shape[1:], lambda s: (s, 0, 0)),
        ],
        out_shape=[
            sds((tokens, width), F32),
            sds((3, width, width), BF),
            sds((8, width), F32),
            sds(table_shape, F32),
        ],
        scratch_shapes=[
            pltpu.VMEM((width, tokens), BF),
            pltpu.VMEM((per, tokens, tokens), BF),
        ],
        compiler_params=pltpu.CompilerParams(vmem_limit_bytes=56 * 2**20),
        name="attend_backward_%d" % layer,
    )(entry, do, o, qn, kn, v, iq, ik, rinv, p, vec, w_qkv, w_qkv, w_qkv, dz)


def entry_logs(first, count, window):
    at = first + lax.broadcasted_iota(jnp.int32, (8, count), 1)
    row = at // (2 * window)
    col = at % (2 * window)
    real = (row < 2 * window - 1) & (col < 2 * window - 1)
    def logs(offset):
        size = jnp.log2(jnp.abs(offset).astype(F32) * (8.0 / (window - 1)) + 1.0) / 3.0
        return jnp.where(offset < 0, -size, size)
    by_row = jnp.where(real, logs(window - 1 - row), 0.0)
    by_col = jnp.where(real, logs(col - (window - 1)), 0.0)
    return by_row, by_col, real


def column_of(token_col, window, shifted):
    if not shifted:
        return token_col
    return jnp.where(token_col >= window // 2, token_col - window // 2, token_col + window // 2)


def table_kernel(window, shifted, chunk, w_ref, out_w_ref, rows_ref, tab_ref, hid_ref, slope_ref):
    step = pl.program_id(0)
    steps = pl.num_programs(0)
    heads = tab_ref.shape[0]
    by_row, by_col, _ = entry_logs(step * chunk, chunk, window)
    pre = w_ref[:, 0:1] * by_row[0:1] + w_ref[:, 1:2] * by_col[0:1] + w_ref[:, 2:3]
    cdf, density = normal_parts(pre)
    act = pre * cdf
    hidden = act.astype(BF)
    hid_ref[...] = hidden
    slope_ref[...] = (cdf + pre * density).astype(BF)
    rest = (act - hidden.astype(F32)).astype(BF)
    both = mm(out_w_ref[...], hidden)
    logits = both[:heads] + both[heads:] + mm(out_w_ref[:heads], rest)
    tab_ref[:, pl.ds(pl.multiple_of(step * chunk, chunk), chunk)] = 16.0 / (1.0 + jnp.exp(-logits))

    @pl.when(step == steps - 1)
    def _():
        spans = tab_ref.shape[1] // LANES
        wide = rows_ref.shape[2]
        row8 = lax.broadcasted_iota(jnp.int32, (8, LANES), 0)
        lane = lax.broadcasted_iota(jnp.int32, (8, LANES), 1)
        for tile in range(window // 8):
            c1 = column_of(row8 + 8 * tile, window, shifted)
            for k in range(wide // LANES):
                at = lane + LANES * k
                m = at // window
                source = 2 * window * m + c1 - column_of(at % window, window, shifted) + window - 1
                low = 2 * window * (LANES * k // window) // LANES
                high = min((2 * window * ((LANES * k + LANES - 1) // window) + 2 * window - 2) // LANES, spans - 1)
                for h in range(heads):
                    got = jnp.zeros((8, LANES), F32)
                    for s in range(low, high + 1):
                        piece = jnp.broadcast_to(tab_ref[h : h + 1, s * LANES : (s + 1) * LANES], (8, LANES))
                        near = source - s * LANES
                        inside = (near >= 0) & (near < LANES)
                        picked = jnp.take_along_axis(piece, jnp.where(inside, near, 0), axis=1)
                        got = jnp.where(inside, picked, got)
                    rows_ref[h, 8 * tile : 8 * tile + 8, k * LANES : (k + 1) * LANES] = got * LOG2E


def bias_table(layer, weights, out_weights, window, shifted):
    hidden, heads = weights.shape[0], out_weights.shape[0] // 2
    entries = 4 * window * window
    chunk = 256
    wide = ((2 * window - 1) * window + LANES - 1) // LANES * LANES
    whole = lambda shape: pl.BlockSpec(shape, lambda s: (0,) * len(shape))
    by_chunk = pl.BlockSpec((hidden, chunk), lambda s: (0, s))
    sds = jax.ShapeDtypeStruct
    return pl.pallas_call(
        functools.partial(table_kernel, window, shifted, chunk),
        grid=(entries // chunk,),
        in_specs=[whole(weights.shape), whole(out_weights.shape)],
        out_specs=[whole((heads, window, wide)), whole((heads, entries)), by_chunk, by_chunk],
        out_shape=[
            sds((heads, window, wide), F32), sds((heads, entries), F32),
            sds((hidden, entries), BF), sds((hidden, entries), BF),
        ],
        compiler_params=pltpu.CompilerParams(vmem_limit_bytes=40 * 2**20),
        name="bias_table_%d" % layer,
    )(weights, out_weights)


def table_back_kernel(window, shifted, chunk, rows_ref, tab_ref, hid_ref, slope_ref, out_w_ref, grads_ref, outs_ref, dlog_s):
    step = pl.program_id(0)
    heads, entries = tab_ref.shape

    @pl.when(step == 0)
    def _():
        grads_ref[...] = jnp.zeros_like(grads_ref)
        outs_ref[...] = jnp.zeros_like(outs_ref)
        spans = rows_ref.shape[2] // LANES
        row8 = lax.broadcasted_iota(jnp.int32, (8, LANES), 0)
        lane = lax.broadcasted_iota(jnp.int32, (8, LANES), 1)
        for k in range(entries // LANES):
            at = lane + LANES * k
            m = at // (2 * window)
            d = at % (2 * window)
            sums = [jnp.zeros((8, LANES), F32) for _ in range(heads)]
            for tile in range(window // 8):
                c1 = column_of(row8 + 8 * tile, window, shifted)
                c2 = c1 - d + window - 1
                real = (c2 >= 0) & (c2 < window) & (m < 2 * window - 1)
                source = window * m + column_of(c2, window, shifted)
                low = window * (LANES * k // (2 * window)) // LANES
                high = min((window * ((LANES * k + LANES - 1) // (2 * window)) + window - 1) // LANES, spans - 1)
                for s in range(low, high + 1):
                    near = source - s * LANES
                    inside = (near >= 0) & (near < LANES) & real
                    near = jnp.where(inside, near, 0)
                    for h in range(heads):
                        piece = rows_ref[h, 8 * tile : 8 * tile + 8, s * LANES : (s + 1) * LANES]
                        picked = jnp.take_along_axis(piece, near, axis=1)
                        sums[h] = sums[h] + jnp.where(inside, picked, 0.0)
            for h in range(heads):
                dlog_s[h : h + 1, k * LANES : (k + 1) * LANES] = jnp.sum(sums[h], axis=0, keepdims=True)
        tab = tab_ref[...]
        dlog_s[...] = dlog_s[...] * tab * (1.0 - tab * 0.0625)

    by_row, by_col, real = entry_logs(step * chunk, chunk, window)
    dlog = dlog_s[:, pl.ds(pl.multiple_of(step * chunk, chunk), chunk)]
    low = dlog.astype(BF)
    outs_ref[...] += mm_nt(hid_ref[...], low)
    dhid = mm_tn(out_w_ref[...], low)
    dpre = (dhid * slope_ref[...].astype(F32)).astype(BF)
    which = lax.broadcasted_iota(jnp.int32, (16, chunk), 0)
    pick = lambda y: jnp.broadcast_to(y[0:1], (16, chunk))
    high_row = by_row.astype(BF).astype(F32)
    high_col = by_col.astype(BF).astype(F32)
    factors = jnp.where(which == 0, pick(high_row), 0.0)
    factors = jnp.where(which == 1, pick(high_col), factors)
    factors = jnp.where(which == 2, 1.0, factors)
    factors = jnp.where(which == 3, pick(by_row - high_row), factors)
    factors = jnp.where(which == 4, pick(by_col - high_col), factors)
    grads_ref[...] += mm_nt(dpre, factors.astype(BF))


def bias_table_backward(layer, rows, tab, hid, slope, out_weights, window, shifted):
    heads, entries = tab.shape
    hidden = hid.shape[0]
    chunk = 256
    whole = lambda shape: pl.BlockSpec(shape, lambda s: (0,) * len(shape))
    by_chunk = pl.BlockSpec((hidden, chunk), lambda s: (0, s))
    sds = jax.ShapeDtypeStruct
    return pl.pallas_call(
        functools.partial(table_back_kernel, window, shifted, chunk),
        grid=(entries // chunk,),
        in_specs=[whole(rows.shape), whole(tab.shape), by_chunk, by_chunk, whole(out_weights.shape)],
        out_specs=[whole((hidden, 16)), whole((hidden, heads))],
        out_shape=[sds((hidden, 16), F32), sds((hidden, heads), F32)],
        scratch_shapes=[pltpu.VMEM((heads, entries), F32)],
        compiler_params=pltpu.CompilerParams(vmem_limit_bytes=40 * 2**20),
        name="bias_table_backward_%d" % layer,
    )(rows, tab, hid, slope, out_weights)


def net_weights(steps, span, weight_in, bias_in):
    down, across = steps
    straight = jnp.abs(down) == span
    by_rows = jnp.where(straight, weight_in[0], weight_in[1]) * jnp.where(down > 0, 1.0, -1.0)
    by_cols = jnp.where(straight, weight_in[1], weight_in[0]) * jnp.where(across > 0, 1.0, -1.0)
    return jnp.pad(jnp.stack([by_rows, by_cols, bias_in], axis=1), ((0, 0), (0, 5)))


def split_out(weight_out):
    turned = weight_out.T
    high = turned.astype(BF)
    return jnp.concatenate([high, (turned - high.astype(F32)).astype(BF)], axis=0)


def net_grads(steps, span, grads, outs):
    down, across = steps
    straight = jnp.abs(down) == span
    by_rows = (grads[:, 0] + grads[:, 3]) * jnp.where(down > 0, 1.0, -1.0)
    by_cols = (grads[:, 1] + grads[:, 4]) * jnp.where(across > 0, 1.0, -1.0)
    weight_in = jnp.stack([jnp.where(straight, by_rows, by_cols), jnp.where(straight, by_cols, by_rows)])
    return weight_in, grads[:, 2], outs


def exchange(x, half_rows, by):
    return passed_along(x[:half_rows].astype(BF), "rows", by).astype(F32)


def take_shifted(x):
    half = x.shape[0] // 2
    return jnp.concatenate([x[half:], exchange(x, half, -1)], axis=0)


def give_back(x):
    half = x.shape[0] // 2
    returned = passed_along(x[half:].astype(BF), "rows", 1).astype(F32)
    return jnp.concatenate([returned, x[:half]], axis=0)


def shares(array, images, bands):
    rows, cols = array.shape
    cut = array.reshape(images, rows // images, bands, cols // bands)
    return jnp.transpose(cut, (0, 2, 1, 3)).reshape(images * bands, -1)


def summed_shares(arrays):
    images, bands = lax.axis_size("img"), lax.axis_size("rows")
    joined = jnp.concatenate([shares(array, images, bands) for array in arrays], axis=1)
    mine = lax.psum_scatter(joined, ("img", "rows"), scatter_dimension=0, tiled=True)
    mine = mine.reshape(-1).astype(F32)
    out = []
    at = 0
    for array in arrays:
        rows, cols = array.shape[0] // images, array.shape[1] // bands
        out.append(mine[at : at + rows * cols].reshape(rows, cols))
        at += rows * cols
    return out


def per_device(
    inputs,
    cotangent,
    region,
    rel_index,
    qkv_weight,
    qv_bias,
    logit_scale,
    place_in,
    place_bias,
    place_out,
    proj_weight,
    up_weight,
    up_bias,
    down_weight,
    out_bias,
    norm_gain,
    norm_shift,
):
    window, width = inputs.shape[2], inputs.shape[3]
    heads = logit_scale.shape[1]
    depth = width // heads
    tokens = window * window
    x = inputs.reshape(tokens, width)
    steps = (rel_index[window, 0] - rel_index[0, 0], rel_index[1, 0] - rel_index[0, 0])
    scales = jnp.repeat(jnp.exp(logit_scale), depth, axis=1)
    vecs = []
    for b in (0, 1):
        rows = [
            qv_bias[b, 0], jnp.zeros_like(qv_bias[b, 0]), qv_bias[b, 1],
            out_bias[b, 0], norm_gain[b, 0], norm_shift[b, 0],
            out_bias[b, 1], norm_gain[b, 1], norm_shift[b, 1], scales[b],
        ]
        vecs.append(jnp.pad(jnp.stack(rows), ((0, 6), (0, 0))))
    up_bias3 = up_bias[:, None, :]
    labels = jnp.roll(region.reshape(window, window), window // 2, axis=1).reshape(tokens, 1)
    same = labels == jnp.arange(LANES)
    low_labels = (
        same.astype(BF),
        jnp.where(same | (jnp.arange(LANES) >= 8), 0.0, -MASKED).astype(BF),
    )

    span = 2 * window - 1
    outs_low = [split_out(place_out[b]) for b in (0, 1)]

    def table_of(b):
        weights = net_weights(steps, span, place_in[b], place_bias[b])
        return bias_table(b, weights, outs_low[b], window, b == 1)

    table_zero, *net_zero = table_of(0)
    table_one, *net_one = table_of(1)

    def forward(b, x, table, masks):
        return block_forward(
            b, x, vecs[b], table, masks, qkv_weight, proj_weight, up_weight,
            up_bias3, down_weight, window, heads,
        )

    def backward(b, dy, saved):
        entry, qn, kn, v, o, iq, ik, rinv, p, a, zr, g, gd, m = saved
        down_grad, up_grad, ub_grad, proj_grad, do, dz, sums = feed_backward(
            b, dy, m, a, zr, o, g, gd, vecs[b], down_weight, up_weight, proj_weight
        )
        first = summed_shares((proj_grad, up_grad, down_grad))
        rows_shape = (heads, window, ((2 * window - 1) * window + LANES - 1) // LANES * LANES)
        dx, qkv3, qsums, table_grad = attend_backward(
            b, entry, do, (qn, kn, v, o, iq, ik, rinv, p), vecs[b], qkv_weight, dz, rows_shape, window, heads
        )
        qkv_grad = jnp.transpose(qkv3, (1, 0, 2)).reshape(width, 3 * width)
        second = summed_shares((qkv_grad,))
        matrices = second + first
        vectors = (
            qsums[0].reshape(heads, depth).sum(axis=1),
            ub_grad.reshape(-1),
            jnp.stack([qsums[1], qsums[3]]),
            jnp.stack([sums[3], sums[0]]),
            jnp.stack([sums[4], sums[1]]),
            jnp.stack([sums[5], sums[2]]),
        )
        return dx, matrices, vectors, table_grad

    band = lambda y: y.reshape(window, window, width)
    flat = lambda y: y.reshape(tokens, width)
    hidden, *saved_zero = forward(0, x, table_zero, None)
    x_one = flat(take_shifted(band(hidden)))
    dy_one = flat(take_shifted(band(cotangent.reshape(tokens, width))))
    shifted_out, *saved_one = forward(1, x_one, table_one, low_labels)
    output = give_back(band(shifted_out)).reshape(inputs.shape)
    dx_one, matrices_one, vectors_one, rows_one = backward(1, dy_one, saved_one)
    dy_zero = flat(give_back(band(dx_one)))
    dx_zero, matrices_zero, vectors_zero, rows_zero = backward(0, dy_zero, saved_zero)

    def pull(b, rows, net):
        grads = bias_table_backward(b, rows, *net, outs_low[b][:heads], window, b == 1)
        return net_grads(steps, span, *grads)

    net_zero = pull(0, rows_zero, net_zero)
    net_one = pull(1, rows_one, net_one)
    small = tuple(
        jnp.stack([first, second])
        for first, second in zip(vectors_zero + net_zero, vectors_one + net_one)
    )
    scale_grad, up_bias_grad, qv_grad, out_bias_grad, gain_grad, shift_grad, in_grad, bias_grad, out_grad = lax.psum(
        small, ("img", "rows")
    )
    qkv_grad, proj_grad, up_grad, down_grad = (
        jnp.stack([first, second]) for first, second in zip(matrices_zero, matrices_one)
    )
    return (
        output,
        dx_zero.reshape(inputs.shape),
        qkv_grad,
        qv_grad,
        scale_grad,
        in_grad,
        bias_grad,
        out_grad,
        proj_grad,
        up_grad,
        up_bias_grad,
        down_grad,
        out_bias_grad,
        gain_grad,
        shift_grad,
    )


def solution(mesh):
    token = P("img", "rows", None, None)
    matrix = P(None, "img", "rows")
    return jax.shard_map(
        per_device,
        mesh=mesh,
        in_specs=(token, token, P("img", "rows", None)) + (P(),) * 14,
        out_specs=(
            token, token, matrix, P(), P(), P(), P(), P(), matrix, matrix, P(), matrix, P(), P(), P(),
        ),
        check_vma=False,
    )
```

time: 6880 us -> 654 us (0.10)
  other arithmetic: 3560 us -> 25.3 us
  local copies, waits for them, and re-layouts: 2600 us -> 107 us
  matrix products: 353 us -> 0 us
  Pallas kernels: 0 us -> 174 us
    scatter-add x2 -> x0, other arithmetic: 3510 us -> none  [position_bias(): return heads_first[:, rel_index]]
    gather x4 -> x0, local copies, waits for them, and re-layouts: 2370 us -> none  [position_bias(): return heads_first[:, rel_index]]
    dot_general x44 -> x0, matrix products: 269 us -> none  [the longest x6 49.7 us: position_bias(): jnp.dot(hidden_net, weight_out, precision=HIGH)]
    reduce_scatter x7 -> x0, waiting for transfers between devices: 239 us -> none  [the longest x1 76.3 us: per_device(): lax.psum_scatter(partial_rows[2], 'img', scatter_dimension=1, tiled=True)]
    pallas_call x0 -> x10, Pallas kernels: none -> 174 us  [the longest x2 59.2 us: block_forward(): pl.pallas_call(kernel, grid=(groups + chunks,), in_specs=[whole((tokens,...]
    mul x4 -> x0, local copies, waits for them, and re-layouts: 169 us -> none  [the longest x2 168 us: attend_back(): probs * (grad_probs - jnp.sum(grad_probs * probs, axis=-1, keepdims=True))]
    unnamed x10 -> x3, waiting for transfers between devices: 0.15 us -> 159 us
    psum x1, waiting for transfers between devices: 25.9 us -> 111 us  [per_device(): lax.psum(small, ('img', 'rows'))]
  transfers between devices with their start and end apart: 13 -> 6, of which waited for: 8 -> 2; matrix products, arithmetic and copies ran while one was open for 73% -> 10% of each run, Pallas kernels for 0% -> 4%
where the time goes in v1:
time: 654 us; the launch traced here: 643 us
  waiting for transfers between devices  270 us (41%)
  Pallas kernels  174 us (27%)
  local copies, waits for them, and re-layouts  107 us (16%)
  blocking collectives  44 us (7%)
  other arithmetic  25.3 us (4%)
  between operations  17.8 us (3%)
    unnamed x3, waiting for transfers between devices  159 us
    psum x1, waiting for transfers between devices, per_device(): lax.psum(small, ('img', 'rows'))  111 us
    pallas_call x2, Pallas kernels, block_forward(): pl.pallas_call(kernel, grid=(groups + chunks,), in_specs=[whole((tokens,...  59.2 us
    pallas_call x2, Pallas kernels, attend_backward(): pl.pallas_call(functools.partial(attend_back_kernel, window, depth, group...  46.6 us
    psum x1, blocking collectives, per_device(): lax.psum(small, ('img', 'rows'))  44 us
    unnamed x57, local copies, waits for them, and re-layouts  31.2 us
    pallas_call x2, Pallas kernels, feed_backward(): pl.pallas_call(functools.partial(feed_back_kernel, chunks), grid=(chunks,...  30.5 us
    reshape x12, local copies, waits for them, and re-layouts, shares(): cut = array.reshape(images, rows // images, bands, cols // bands)  28.2 us
  transfers between devices with their start and end apart: 6, of which 2 were waited for; matrix products, arithmetic and copies ran while one was open for 10% of the time, Pallas kernels for 4%

profile of v1, /device:TPU:0, one launch (start us, length us, event | category | flops | bytes accessed | tf_op | source)
XLA Modules:
  0.0 643.0 jit_solution(3133974555776454191)
XLA Ops:
  7.2 1.3 fusion.13
  16.9 1.3 broadcast_in_dim.28.ub_ref
  18.3 11.6 %bias_table_0.1 = (f32[16,24,1152]{2,1,0:T(8,128)S(1)}, f32[16,2304]{1,0:T(8,128)S(1)}, bf16[512,2304]{1,0:T(8,128)(2,1)S(1)}, bf16[512,2304]{1,0:T(8,128)(2,1)S(1)}) custom-call(f32[512,8]{1,0:T(8,128)S(1)} %pad.15.w_ref, bf16[32,512]{1,0:T(8,128)(2,1)S(1)} %get-tuple-element.273.out_w_ref), custom_call_target="tpu_custom_call" | custom-call | tf_op jit(solution)/shard_map/bias_table_0/pallas_call | solution.py:492
  29.9 1.5 copy-done
  31.4 1.2 copy-done.7
  33.2 29.6 %block_forward_0.1 = (f32[576,512]{1,0:T(8,128)}, bf16[576,512]{1,0:T(8,128)(2,1)}, bf16[576,512]{1,0:T(8,128)(2,1)}, bf16[576,512]{1,0:T(8,128)(2,1)}, bf16[576...) custom-call(f32[576,512]{1,0:T(8,128)} %bitcast.179, ...), custom_call_target="tpu_custom_call" | custom-call | tf_op jit(solution)/shard_map/block_forward_0/pallas_call | solution.py:187
  62.8 1.8 slice.458
  64.6 3.0 collective-permute-start
  70.2 1.9 slice.295
  73.2 11.8 %bias_table_1.1 = (f32[16,24,1152]{2,1,0:T(8,128)S(1)}, f32[16,2304]{1,0:T(8,128)S(1)}, bf16[512,2304]{1,0:T(8,128)(2,1)S(1)}, bf16[512,2304]{1,0:T(8,128)(2,1)S(1)}) custom-call(f32[512,8]{1,0:T(8,128)S(1)} %pad.17.w_ref, bf16[32,512]{1,0:T(8,128)(2,1)S(1)} %get-tuple-element.274.out_w_ref), custom_call_target="tpu_custom_call" | custom-call | tf_op jit(solution)/shard_map/bias_table_1/pallas_call | solution.py:492
  85.1 1.4 copy-done.4
  87.4 1.3 convert_element_type.96
  88.7 2.2 pad_maximum_fusion.2
  91.0 1.1 pad_maximum_fusion.3
  92.1 29.6 %block_forward_1.1 = (f32[576,512]{1,0:T(8,128)}, bf16[576,512]{1,0:T(8,128)(2,1)}, bf16[576,512]{1,0:T(8,128)(2,1)}, bf16[576,512]{1,0:T(8,128)(2,1)}, bf16[576...) custom-call(f32[576,512]{1,0:T(8,128)} %bitcast.167, ...), custom_call_target="tpu_custom_call" | custom-call | tf_op jit(solution)/shard_map/block_forward_1/pallas_call | solution.py:187
  121.7 15.5 %feed_backward_1.1 = (bf16[2048,512]{1,0:T(8,128)(2,1)}, bf16[512,2048]{1,0:T(8,128)(2,1)}, f32[1,1,2048]{2,1,0:T(1,128)}, bf16[512,512]{1,0:T(8,128)(2,1)}, bf1...) custom-call(f32[576,512]{1,0:T(8,128)} %bitcast.168, f32[576,512]{1,0:T(8,128)} %get-tuple-element.85.m_ref, ...), custom_call_target="tpu_custom_call" | custom-call | tf_op jit(solution)/shard_map/feed_backward_1/pallas_call | solution.py:279
  137.2 23.3 %attend_backward_1.1 = (f32[576,512]{1,0:T(8,128)}, bf16[3,512,512]{2,1,0:T(8,128)(2,1)}, f32[8,512]{1,0:T(8,128)}, f32[16,24,1152]{2,1,0:T(8,128)}) custom-call(bf16[576,512]{1,0:T(8,128)(2,1)} %get-tuple-element.84.e_ref, bf16[576,512]{1,0:T(8,128)(2,1)} %get-tuple-element.91.do_ref, f32[576,512]{1,0:T(8,128)} %get-tuple-element.88.o_ref, ...), custom_call_target="tpu_custom_call" | custom-call | tf_op jit(solution)/shard_map/attend_backward_1/pallas_call | solution.py:392
  160.5 1.8 slice.456
  162.3 2.0 collective-permute-start.3
  164.4 4.5 reshape.453
  168.9 2.2 copy.77
  171.1 2.5 copy.85
  173.6 4.1 reshape.455
  177.7 2.0 copy.78
  179.7 2.6 copy.86
  182.3 1.2 reshape.451
  183.8 1.2 copy-done.12
  185.0 3.6 pad_maximum_fusion.1
  188.7 2.7 copy.69
  191.4 5.8 reshape_reshape.8
  197.2 1.7 copy.70
  198.9 2.0 copy.80
  201.9 1.1 pad_maximum_fusion.4
  203.0 15.1 %feed_backward_0.1 = (bf16[2048,512]{1,0:T(8,128)(2,1)}, bf16[512,2048]{1,0:T(8,128)(2,1)}, f32[1,1,2048]{2,1,0:T(1,128)}, bf16[512,512]{1,0:T(8,128)(2,1)}, bf1...) custom-call(f32[576,512]{1,0:T(8,128)} %bitcast.169, f32[576,512]{1,0:T(8,128)} %get-tuple-element.101.m_ref, ...), custom_call_target="tpu_custom_call" | custom-call | tf_op jit(solution)/shard_map/feed_backward_0/pallas_call | solution.py:279
  218.1 4.5 reshape.447
  222.6 2.2 copy.74
  224.9 2.5 copy.82
  227.4 4.2 reshape.449
  231.6 2.0 copy.75
  233.6 2.5 copy.83
  236.1 1.2 reshape.445
  237.7 23.3 %attend_backward_0.1 = (f32[576,512]{1,0:T(8,128)}, bf16[3,512,512]{2,1,0:T(8,128)(2,1)}, f32[8,512]{1,0:T(8,128)}, f32[16,24,1152]{2,1,0:T(8,128)}) custom-call(bf16[576,512]{1,0:T(8,128)(2,1)} %get-tuple-element.83.e_ref, bf16[576,512]{1,0:T(8,128)(2,1)} %get-tuple-element.107.do_ref, f32[576,512]{1,0:T(8,128)} %get-tuple-element.104.o_ref, ...), custom_call_target="tpu_custom_call" | custom-call | tf_op jit(solution)/shard_map/attend_backward_0/pallas_call | solution.py:392
  261.0 4.1 copy.67
  265.1 5.8 reshape_reshape.7
  270.9 1.9 copy.68
  272.7 2.0 copy.79
  274.8 2.3 pad_maximum_fusion
  277.1 2.0 slice.457
  279.1 1.9 slice.315
  281.0 1.7 copy-done.3
  282.7 2.1 copy-done.5
  284.8 7.3 %bias_table_backward_1.1 = (f32[512,16]{1,0:T(8,128)S(1)}, f32[512,16]{1,0:T(8,128)S(1)}) custom-call(f32[16,24,1152]{2,1,0:T(8,128)S(1)} %copy-done.8, f32[16,2304]{1,0:T(8,128)S(1)} %get-tuple-element.127.tab_ref, bf16[512,2304]{1,0:T(8,128)(2,1)S(1)} %copy-done.3, bf16[512,2304]{1,0:T(8,128)(2,1)S(1)} %copy-done.5, ...), custom_call_target="tpu_custom_call" | custom-call | tf_op jit(solution)/shard_map/bias_table_backward_1/pallas_call | solution.py:567
  294.0 1.7 copy-done.1
  295.7 1.5 copy-done.9
  297.2 7.0 %bias_table_backward_0.1 = (f32[512,16]{1,0:T(8,128)S(1)}, f32[512,16]{1,0:T(8,128)S(1)}) custom-call(f32[16,24,1152]{2,1,0:T(8,128)S(1)} %copy-done.9, f32[16,2304]{1,0:T(8,128)S(1)} %get-tuple-element.122.tab_ref, bf16[512,2304]{1,0:T(8,128)(2,1)S(1)} %get-tuple-element.123.hid_ref, bf16[512,2304]{1,0:T(8,128)(2,1)S(1)} %copy-done.1, ...), custom_call_target="tpu_custom_call" | custom-call | tf_op jit(solution)/shard_map/bias_table_backward_0/pallas_call | solution.py:567
  307.0 1.1 maximum_bitcast_fusion
  308.1 44.0 %all-reduce.8 = (f32[2,2,512]{2,1,0:T(2,128)}, f32[2,16]{1,0:T(2,128)}, f32[2,2,512]{2,1,0:T(2,128)}, f32[2,512]{1,0:T(2,128)}, f32[2,2048]{1,0:T(2,128)}, /*ind...) all-reduce(f32[2,2,512]{2,1,0:T(2,128)S(1)} %pad_maximum_fusion.13,, ...), channel_id=1, replica_groups=mesh['img'=16,'rows'=2] {'img','rows'}, use_global_device_ids=true, to_apply=%region_2.3 | all-reduce | flops 15392 | bytes 123136 | tf_op jit(solution)/shard_map/psum | solution.py:739
  352.1 158.7 %all-reduce.15.cloned.1.call-done = (bf16[32,24576]{1,0:T(8,128)(2,1)}, bf16[32,24576]{1,0:T(8,128)(2,1)}, bf16[32,73728]{1,0:T(8,128)(2,1)}, bf16[32,73728]{1,0:T(8,128)(2,1)}) async-done(((bf16[32,24576]{1,0:T(8,128)(2,1)}, bf16[32,24576]{1,0:T(8,128)(2,1)}, bf16[32,73728]{1,0:T(8,128)(2,1)}, bf16[32,73728]{1,0:T(8,128)(2,1)}), (bf16[32,24576]{1,0:T(8,128)(2,1)}, bf16[32,24576]{1,0:T(8,128)(2,1)}, ...) | async-done | bytes 12582928
  510.7 1.5 dynamic-slice_convert_fusion.1
  513.3 1.5 dynamic-slice_convert_fusion
  517.3 1.3 dynamic-slice_reduce_fusion.1
  518.7 1.3 dynamic-slice_reduce_fusion
  522.8 111.4 %all-reduce.13.cloned.1.call-done = f32[2,512,16]{1,2,0:T(8,128)} async-done(((f32[2,512,16]{1,2,0:T(8,128)}), f32[2,512,16]{1,2,0:T(8,128)}) %all-reduce.13.cloned.1.call-update) | async-done | bytes 65552 | tf_op jit(solution)/shard_map/psum | solution.py:739
  634.2 1.5 copy.92
  (134 shorter events, 23.8 us)
Async XLA Ops:
  7.2 503.6 %all-reduce.15.cloned.1.call-start = ((), (), s32[]{:S(2)}) async-start(), calls=%async_computation.1 | async-start | bytes 25165824
  29.9 1.5 copy-start
  31.4 1.2 copy-start.7
  33.2 34.4 %copy-start.16 = (f32[1,24,24,512]{3,2,1,0:T(8,128)S(1)}, f32[1,24,24,512]{3,2,1,0:T(8,128)}, u32[]{:S(2)}) copy-start(f32[1,24,24,512]{3,2,1,0:T(8,128)} %param.18) | copy-start | bytes 3538948
  62.8 6.4 copy-start.18
  64.6 22.8 %collective-permute-start = (bf16[12,24,512]{2,1,0:T(8,128)(2,1)}, bf16[12,24,512]{2,1,0:T(8,128)(2,1)}, u32[]{:S(2)}, u32[]{:S(2)}) collective-permute-start(bf16[12,24,512]{2,1,0:T(8,128)(2,1)} %bitcast.20), channel_id=1, source_target_pairs={{0,1},{1,0},{2,3},{3,2},{4,5},{5,4},{6,7},{7,6},{8,9},{9,8},{10,11... | collective-permute-start | bytes 884744 | tf_op jit(solution)/shard_map/ppermute | solution.py:19
  68.3 22.6 %collective-permute-start.2 = (bf16[12,24,512]{2,1,0:T(8,128)(2,1)}, bf16[12,24,512]{2,1,0:T(8,128)(2,1)S(1)}, u32[]{:S(2)}, u32[]{:S(2)}) collective-permute-start(bf16[12,24,512]{2,1,0:T(8,128)(2,1)} %fusion), channel_id=1, source_target_pairs={{0,1},{1,0},{2,3},{3,2},{4,5},{5,4},{6,7},{7,6},{8,9},{9,8},{10,11... | collective-permute-start | bytes 884744 | tf_op jit(solution)/shard_map/ppermute | solution.py:19
  85.0 1.4 copy-start.4
  86.5 4.5 copy-start.2
  86.5 4.5 copy-start.6
  87.4 3.6 copy-start.14
  162.3 38.6 %collective-permute-start.3 = (bf16[12,24,512]{2,1,0:T(8,128)(2,1)}, bf16[12,24,512]{2,1,0:T(8,128)(2,1)}, u32[]{:S(2)}, u32[]{:S(2)}) collective-permute-start(bf16[12,24,512]{2,1,0:T(8,128)(2,1)} %bitcast.44), channel_id=1, source_target_pairs={{0,1},{1,0},{2,3},{3,2},{4,5},{5,4},{6,7},{7,6},{8,9},{9,8},{10,11... | collective-permute-start | bytes 884744 | tf_op jit(solution)/shard_map/ppermute | solution.py:19
  183.4 1.6 copy-start.12
  185.0 3.6 copy-start.17
  185.0 3.7 copy-start.15
  270.9 3.9 copy-start.11
  272.7 2.1 copy-start.10
  277.1 357.2 %all-reduce.13.cloned.1.call-start = ((), (), s32[]{:S(2)}) async-start(), calls=%async_computation | async-start | bytes 131072 | tf_op jit(solution)/shard_map/psum | solution.py:739
  277.1 3.9 copy-start.8
  281.0 1.7 copy-start.3
  282.7 2.1 copy-start.5
  284.8 8.5 %copy-start.19 = (f32[8,512]{1,0:T(8,128)S(1)}, f32[8,512]{1,0:T(8,128)}, u32[]{:S(2)}) copy-start(f32[8,512]{1,0:T(8,128)} %get-tuple-element.142) | copy-start | bytes 49156
  293.2 13.7 %collective-permute-start.1 = (bf16[12,24,512]{2,1,0:T(8,128)(2,1)}, bf16[12,24,512]{2,1,0:T(8,128)(2,1)S(1)}, u32[]{:S(2)}, u32[]{:S(2)}) collective-permute-start(bf16[12,24,512]{2,1,0:T(8,128)(2,1)} %bitcast.180), channel_id=1, source_target_pairs={{0,1},{1,0},{2,3},{3,2},{4,5},{5,4},{6,7},{7,6},{8,9},{9,8},{10,11... | collective-permute-start | bytes 884744 | tf_op jit(solution)/shard_map/ppermute | solution.py:19
  294.0 1.7 copy-start.1
  295.7 1.5 copy-start.9
  297.2 9.4 %copy-start.20 = (f32[8,512]{1,0:T(8,128)S(1)}, f32[8,512]{1,0:T(8,128)}, u32[]{:S(2)}) copy-start(f32[8,512]{1,0:T(8,128)} %get-tuple-element.141) | copy-start | bytes 49156
  297.2 9.7 %copy-start.21 = (f32[1,1,2048]{2,1,0:T(1,128)S(1)}, f32[1,1,2048]{2,1,0:T(1,128)}, u32[]{:S(2)}) copy-start(f32[1,1,2048]{2,1,0:T(1,128)} %get-tuple-element.140) | copy-start | bytes 24580
  297.2 9.7 %copy-start.22 = (f32[1,1,2048]{2,1,0:T(1,128)S(1)}, f32[1,1,2048]{2,1,0:T(1,128)}, u32[]{:S(2)}) copy-start(f32[1,1,2048]{2,1,0:T(1,128)} %get-tuple-element.139) | copy-start | bytes 24580
  304.3 2.7 copy-start.13
Sparse Core Ops, SparseCore 0:
  277.2 233.4 all-reduce.14
  516.9 117.2 all-reduce.12
